TPU v7x, 256 devices: a whole 4x4x8 slice. The times are simulated.
256 devices in a mesh: blk: 128 (over z_hi, y, x, core), rep: 2 (over z_lo).
Axes of the slice: x: 4, y: 4, z: 8 (z_hi: 4, z_lo: 2; z = z_hi * 2 + z_lo), core: 2. Of those that a mesh axis runs over, the one named last changes fastest.
Arguments:
- fwd_in: bfloat16 [114688, 1024], P(('blk', 'rep')), may hold values from -6 to 6
- bwd_in: bfloat16 [114688, 1024], P(('blk', 'rep')), may hold values from -6 to 6
- cotangent: bfloat16 [114688, 1024], P(('blk', 'rep')), may hold values from -6 to 6
- w_in: bfloat16 [1024, 65536], P(None, 'blk'), may hold values from -0.1875 to 0.1875
- w_out: bfloat16 [65536, 1024], P('blk'), may hold values from -0.125 to 0.125
Outputs:
- forward_out: bfloat16 [114688, 1024], P(('blk', 'rep'))
- input_grad: bfloat16 [114688, 1024], P(('blk', 'rep'))
- in_grad: float32 [1024, 65536], P('rep', 'blk')
- down_grad: float32 [65536, 1024], P('blk', 'rep')
All inputs are finite; a program needn't handle non-finite values.
Results may differ from a plain program's by a relative error of at most 0.0066.
Values may be sent and summed in bfloat16 or wider, within the bound.
A program may use at most 128 MiB of HBM per device.

v0:
```python
import jax
import jax.numpy as jnp
from jax import lax
from jax.sharding import PartitionSpec as P

TICKS = 4


def from_behind(value, axis, steps):
    count = lax.axis_size(axis)
    pairs = [(source, (source + steps) % count) for source in range(count)]
    return lax.ppermute(value, axis, pairs)


def shortened(value):

    def short(part):
        return part.astype(jnp.bfloat16) if part.dtype == jnp.float32 else part

    return jax.tree.map(short, value)


def split_up(value, dim, count):
    shape = value.shape
    tiles = value.reshape(*shape[:dim], count, shape[dim] // count, *shape[dim + 1 :])
    return jnp.moveaxis(tiles, dim, 0)


def summed_on_arrival(value, axis, dim):
    tiles = split_up(value, dim, lax.axis_size(axis))
    arrived = lax.all_to_all(tiles, axis, split_axis=0, concat_axis=0, tiled=True)
    return arrived.astype(jnp.float32).sum(axis=0)


def inner(left, right, left_dim, right_dim):
    return lax.dot_general(
        left, right, (((left_dim,), (right_dim,)), ((), ())), preferred_element_type=jnp.float32
    )


def backward_pieces(inputs, cotan, w_in_slot, w_out_slot):
    preact = jnp.dot(inputs, w_in_slot, preferred_element_type=jnp.float32)
    active, pullback = jax.vjp(jax.nn.gelu, preact)
    hidden = active.astype(jnp.bfloat16)
    hid_grad = inner(cotan, w_out_slot, 1, 1)
    pre_grad = pullback(hid_grad)[0].astype(jnp.bfloat16)
    return (hidden, pre_grad)


def on_device(fwd_in, bwd_in, cotangent, w_in, w_out):
    slot_list = [(w_in, w_out)]
    for tick in range(1, TICKS):
        slot_list.append(from_behind((w_in, w_out), "blk", tick))
    fwd_sum = jnp.zeros((fwd_in.shape[0], fwd_in.shape[1]), jnp.float32)
    grad_sum = jnp.zeros((bwd_in.shape[0], bwd_in.shape[1]), jnp.float32)
    partials = []
    for w_in_slot, w_out_slot in slot_list:
        preact = jnp.dot(fwd_in, w_in_slot, preferred_element_type=jnp.float32)
        fwd_sum = fwd_sum + jnp.dot(
            jax.nn.gelu(preact).astype(jnp.bfloat16), w_out_slot, preferred_element_type=jnp.float32
        )
        hidden, pre_grad = backward_pieces(bwd_in, cotangent, w_in_slot, w_out_slot)
        grad_sum = grad_sum + inner(pre_grad, w_in_slot, 1, 1)
        partials.append((inner(bwd_in, pre_grad, 0, 0), inner(hidden, cotangent, 0, 0)))
    running = partials[TICKS - 1]
    for tick in range(TICKS - 2, -1, -1):
        arrived = jax.tree.map(
            lambda part, own: part.astype(own.dtype),
            from_behind(shortened(running), "blk", -1),
            running,
        )
        running = (arrived[0] + partials[tick][0], arrived[1] + partials[tick][1])
    in_grad, down_grad = (
        summed_on_arrival(running[0].astype(jnp.bfloat16), "rep", 0),
        summed_on_arrival(running[1].astype(jnp.bfloat16), "rep", 1),
    )
    return (fwd_sum.astype(jnp.bfloat16), grad_sum.astype(jnp.bfloat16), in_grad, down_grad)


def solution(mesh):
    in_specs = (
        P(("blk", "rep"), None),
        P(("blk", "rep"), None),
        P(("blk", "rep"), None),
        P(None, "blk"),
        P("blk", None),
    )
    out_specs = (P(("blk", "rep"), None), P(("blk", "rep"), None), P("rep", "blk"), P("blk", "rep"))
    return jax.shard_map(
        on_device, mesh=mesh, in_specs=in_specs, out_specs=out_specs, check_vma=False
    )
```

profile of v0, /device:TPU:64, one launch (start us, length us, event | category | flops | bytes accessed | tf_op | source)
XLA Modules:
  0.0 373.3 jit_solution(15838532730765472096)
XLA Ops:
  2.2 2.4 collective-permute-start.5
  12.9 4.3 %fusion.75 = f32[448,1024]{1,0:T(8,128)} fusion(bf16[512,1024]{1,0:T(8,128)(2,1)} %param.9, bf16[448,1024]{1,0:T(8,128)(2,1)} %param.5, bf16[1024,512]{1,0:T(8,128)(2,1)} %param.8), kind=kOutput, calls=%fused_computation.100 | convolution fusion | flops 941588480 | bytes 4849664 | tf_op jit(solution)/shard_map/dot_general | solution.py:59
  17.2 76.3 %collective-permute-done.4 = bf16[1024,512]{1,0:T(8,128)(2,1)} collective-permute-done((bf16[1024,512]{1,0:T(8,128)(2,1)}, bf16[1024,512]{1,0:T(8,128)(2,1)}, u32[]{:S(2)}, u32[]{:S(2)}) %collective-permute-start.4) | collective-permute-done | bytes 1048608 | tf_op jit(solution)/shard_map/ppermute | solution.py:12
  93.5 79.5 %collective-permute-start = (bf16[1024,512]{1,0:T(8,128)(2,1)}, bf16[1024,512]{1,0:T(8,128)(2,1)S(1)}, u32[]{:S(2)}, u32[]{:S(2)}) collective-permute-start(bf16[1024,512]{1,0:T(8,128)(2,1)} %param.8), channel_id=1, source_target_pairs={{0,2},{2,4},{4,6},{6,8},{8,10},{10,12},{12,14},{14,16},{16,18},{18... | collective-permute-start | bytes 3145736 | tf_op jit(solution)/shard_map/ppermute | solution.py:12
  174.9 2.4 fusion.31
  178.0 17.0 %collective-permute-start.6 = (bf16[1024,512]{0,1:T(8,128)(2,1)S(1)}, bf16[1024,512]{0,1:T(8,128)(2,1)S(1)}, u32[]{:S(2)}, u32[]{:S(2)}) collective-permute-start(bf16[1024,512]{0,1:T(8,128)(2,1)S(1)} %fusion.3), channel_id=1, source_target_pairs={{0,254},{2,0},{4,2},{6,4},{8,6},{10,8},{12,10},{14,12},{16,14},{18... | collective-permute-start | bytes 3145736 | tf_op jit(solution)/shard_map/ppermute | solution.py:12
  200.4 2.4 fusion.24
  202.8 4.6 %collective-permute-done.6 = bf16[1024,512]{0,1:T(8,128)(2,1)S(1)} collective-permute-done((bf16[1024,512]{0,1:T(8,128)(2,1)S(1)}, bf16[1024,512]{0,1:T(8,128)(2,1)S(1)}, u32[]{:S(2)}, u32[]{:S(2)}) %collective-permute-start.6) | collective-permute-done | bytes 1048608 | tf_op jit(solution)/shard_map/ppermute | solution.py:12
  208.1 7.1 %collective-permute-start.7 = (bf16[1024,512]{0,1:T(8,128)(2,1)S(1)}, bf16[1024,512]{0,1:T(8,128)(2,1)S(1)}, u32[]{:S(2)}, u32[]{:S(2)}) collective-permute-start(bf16[1024,512]{0,1:T(8,128)(2,1)S(1)} %fusion.2), channel_id=1, source_target_pairs={{0,254},{2,0},{4,2},{6,4},{8,6},{10,8},{12,10},{14,12},{16,14},{18... | collective-permute-start | bytes 3145736 | tf_op jit(solution)/shard_map/ppermute | solution.py:12
  215.2 8.4 %collective-permute-done = bf16[1024,512]{1,0:T(8,128)(2,1)S(1)} collective-permute-done((bf16[1024,512]{1,0:T(8,128)(2,1)}, bf16[1024,512]{1,0:T(8,128)(2,1)S(1)}, u32[]{:S(2)}, u32[]{:S(2)}) %collective-permute-start) | collective-permute-done | bytes 1048608 | tf_op jit(solution)/shard_map/ppermute | solution.py:12
  224.3 2.4 fusion.17
  231.3 7.0 %collective-permute-start.8 = (bf16[1024,512]{0,1:T(8,128)(2,1)}, bf16[1024,512]{0,1:T(8,128)(2,1)}, u32[]{:S(2)}, u32[]{:S(2)}) collective-permute-start(bf16[1024,512]{0,1:T(8,128)(2,1)} %fusion.1), channel_id=1, source_target_pairs={{0,254},{2,0},{4,2},{6,4},{8,6},{10,8},{12,10},{14,12},{16,14},{18... | collective-permute-start | bytes 3145736 | tf_op jit(solution)/shard_map/ppermute | solution.py:12
  238.3 3.1 fusion.154
  243.6 4.3 %fusion.71 = f32[448,1024]{1,0:T(8,128)} fusion(bf16[512,1024]{1,0:T(8,128)(2,1)} %collective-permute-done.3, bf16[448,1024]{1,0:T(8,128)(2,1)} %param.5, bf16[1024,512]{1,0:T(8,128)(2,1)} %collective-permute-done.2), kind=kOutput, calls=%fused_computation.98 | convolution fusion | flops 941588480 | bytes 4849664 | tf_op jit(solution)/shard_map/dot_general | solution.py:59
  247.9 58.0 %collective-permute-done.10 = bf16[512,1024]{1,0:T(8,128)(2,1)} collective-permute-done((bf16[512,1024]{1,0:T(8,128)(2,1)}, bf16[512,1024]{1,0:T(8,128)(2,1)}, u32[]{:S(2)}, u32[]{:S(2)}) %collective-permute-start.10) | collective-permute-done | bytes 1048608 | tf_op jit(solution)/shard_map/ppermute | solution.py:12
  305.9 3.2 add_convert_fusion.1
  309.1 7.0 %collective-permute-start.11 = (bf16[512,1024]{1,0:T(8,128)(2,1)}, bf16[512,1024]{1,0:T(8,128)(2,1)}, u32[]{:S(2)}, u32[]{:S(2)}) collective-permute-start(bf16[512,1024]{1,0:T(8,128)(2,1)} %add_convert_fusion.1), channel_id=1, source_target_pairs={{0,254},{2,0},{4,2},{6,4},{8,6},{10,8},{12,10},{14,12},{16,14},{18... | collective-permute-start | bytes 3145736 | tf_op jit(solution)/shard_map/ppermute | solution.py:12
  316.2 4.3 %collective-permute-done.8 = bf16[1024,512]{0,1:T(8,128)(2,1)} collective-permute-done((bf16[1024,512]{0,1:T(8,128)(2,1)}, bf16[1024,512]{0,1:T(8,128)(2,1)}, u32[]{:S(2)}, u32[]{:S(2)}) %collective-permute-start.8) | collective-permute-done | bytes 1048608 | tf_op jit(solution)/shard_map/ppermute | solution.py:12
  323.1 4.5 %all-to-all-start = ((bf16[2,512,512]{1,2,0:T(8,128)(2,1)}), bf16[2,512,512]{1,2,0:T(8,128)(2,1)}, u32[]{:S(2)}, u32[]{:S(2)}) async-start(bf16[2,512,512]{1,2,0:T(8,128)(2,1)} %bitcast.73), calls=%async_computation | async-start | bytes 2097152 | tf_op jit(solution)/shard_map/all_to_all | solution.py:31
  329.8 3.0 add_convert_fusion.3
  335.5 19.6 %all-to-all-done = bf16[2,512,512]{1,2,0:T(8,128)(2,1)} async-done(((bf16[2,512,512]{1,2,0:T(8,128)(2,1)}), bf16[2,512,512]{1,2,0:T(8,128)(2,1)}, u32[]{:S(2)}, u32[]{:S(2)}) %all-to-all-start) | async-done | bytes 1048608 | tf_op jit(solution)/shard_map/all_to_all | solution.py:31
  355.1 3.6 all-to-all-start.1
  358.7 4.0 %fusion.73 = f32[448,1024]{1,0:T(8,128)} fusion(bf16[512,1024]{1,0:T(8,128)(2,1)} %collective-permute-done.1, bf16[448,1024]{1,0:T(8,128)(2,1)} %param.5, bf16[1024,512]{1,0:T(8,128)(2,1)S(1)} %copy-done.7), kind=kOutput, calls=%fused_computation.99 | convolution fusion | flops 941588480 | bytes 4849664 | tf_op jit(solution)/shard_map/dot_general | solution.py:59
  362.8 5.7 %add_convert_fusion.4 = bf16[448,1024]{1,0:T(8,128)(2,1)} fusion(f32[448,1024]{1,0:T(8,128)} %fusion.71, f32[448,1024]{1,0:T(8,128)} %fusion.75, f32[448,1024]{1,0:T(8,128)} %fusion.73, bf16[512,1024]{1,0:T(8,128)(2,1)} %collective-permute-done.5, bf16[448,1024]{1,0:T(8,128)(2,1)} %param.5, bf16[1024,512]{1,0:T(8,128)(2,1)} %collective-permute-done.4), kind=kOutput, calls=%fused_computation.12 | convolution fusion | flops 943423488 | bytes 9437184 | tf_op jit(solution)/shard_map/dot_general | solution.py:59
  (61 shorter events, 38.0 us)
Async XLA Ops:
  0.6 7.7 %copy-start = (bf16[448,1024]{1,0:T(8,128)(2,1)S(1)}, bf16[448,1024]{1,0:T(8,128)(2,1)}, u32[]{:S(2)}) copy-start(bf16[448,1024]{1,0:T(8,128)(2,1)} %param.6) | copy-start | bytes 2752516
  0.6 7.7 %copy-start.4 = (bf16[1024,512]{1,0:T(8,128)(2,1)S(1)}, bf16[1024,512]{1,0:T(8,128)(2,1)}, u32[]{:S(2)}) copy-start(bf16[1024,512]{1,0:T(8,128)(2,1)} %param.8) | copy-start | bytes 3145732
  0.7 199.7 %collective-permute-start.3 = (bf16[512,1024]{1,0:T(8,128)(2,1)}, bf16[512,1024]{1,0:T(8,128)(2,1)}, u32[]{:S(2)}, u32[]{:S(2)}) collective-permute-start(bf16[512,1024]{1,0:T(8,128)(2,1)} %param.9), channel_id=1, source_target_pairs={{0,4},{2,6},{4,8},{6,10},{8,12},{10,14},{12,16},{14,18},{16,20},{1... | collective-permute-start | bytes 3145736 | tf_op jit(solution)/shard_map/ppermute | solution.py:12
  2.2 222.0 %collective-permute-start.1 = (bf16[512,1024]{1,0:T(8,128)(2,1)}, bf16[512,1024]{1,0:T(8,128)(2,1)}, u32[]{:S(2)}, u32[]{:S(2)}) collective-permute-start(bf16[512,1024]{1,0:T(8,128)(2,1)} %param.9), channel_id=1, source_target_pairs={{0,2},{2,4},{4,6},{6,8},{8,10},{10,12},{12,14},{14,16},{16,18},{18... | collective-permute-start | bytes 3145736 | tf_op jit(solution)/shard_map/ppermute | solution.py:12
  2.2 172.7 %collective-permute-start.5 = (bf16[512,1024]{1,0:T(8,128)(2,1)}, bf16[512,1024]{1,0:T(8,128)(2,1)}, u32[]{:S(2)}, u32[]{:S(2)}) collective-permute-start(bf16[512,1024]{1,0:T(8,128)(2,1)} %param.9), channel_id=1, source_target_pairs={{0,6},{2,8},{4,10},{6,12},{8,14},{10,16},{12,18},{14,20},{16,22},{... | collective-permute-start | bytes 3145736 | tf_op jit(solution)/shard_map/ppermute | solution.py:12
  4.6 193.3 %collective-permute-start.2 = (bf16[1024,512]{1,0:T(8,128)(2,1)}, bf16[1024,512]{1,0:T(8,128)(2,1)}, u32[]{:S(2)}, u32[]{:S(2)}) collective-permute-start(bf16[1024,512]{1,0:T(8,128)(2,1)} %param.8), channel_id=1, source_target_pairs={{0,4},{2,6},{4,8},{6,10},{8,12},{10,14},{12,16},{14,18},{16,20},{1... | collective-permute-start | bytes 3145736 | tf_op jit(solution)/shard_map/ppermute | solution.py:12
  6.1 87.4 %collective-permute-start.4 = (bf16[1024,512]{1,0:T(8,128)(2,1)}, bf16[1024,512]{1,0:T(8,128)(2,1)}, u32[]{:S(2)}, u32[]{:S(2)}) collective-permute-start(bf16[1024,512]{1,0:T(8,128)(2,1)} %param.8), channel_id=1, source_target_pairs={{0,6},{2,8},{4,10},{6,12},{8,14},{10,16},{12,18},{14,20},{16,22},{... | collective-permute-start | bytes 3145736 | tf_op jit(solution)/shard_map/ppermute | solution.py:12
  17.2 157.7 %copy-start.11 = (bf16[448,1024]{1,0:T(8,128)(2,1)S(1)}, bf16[448,1024]{1,0:T(8,128)(2,1)}, u32[]{:S(2)}) copy-start(bf16[448,1024]{1,0:T(8,128)(2,1)} %param.7) | copy-start | bytes 2752516
  93.5 130.1 %collective-permute-start = (bf16[1024,512]{1,0:T(8,128)(2,1)}, bf16[1024,512]{1,0:T(8,128)(2,1)S(1)}, u32[]{:S(2)}, u32[]{:S(2)}) collective-permute-start(bf16[1024,512]{1,0:T(8,128)(2,1)} %param.8), channel_id=1, source_target_pairs={{0,2},{2,4},{4,6},{6,8},{8,10},{10,12},{12,14},{14,16},{16,18},{18... | collective-permute-start | bytes 3145736 | tf_op jit(solution)/shard_map/ppermute | solution.py:12
  177.3 19.8 %copy-start.8 = (bf16[448,512]{1,0:T(8,128)(2,1)}, bf16[448,512]{1,0:T(8,128)(2,1)S(1)}, u32[]{:S(2)}) copy-start(bf16[448,512]{1,0:T(8,128)(2,1)S(1)} %fusion.31) | copy-start | bytes 1376260
  177.3 17.8 %copy-start.5 = (bf16[1024,512]{1,0:T(8,128)(2,1)S(1)}, bf16[1024,512]{1,0:T(8,128)(2,1)}, u32[]{:S(2)}) copy-start(bf16[1024,512]{1,0:T(8,128)(2,1)} %param.8) | copy-start | bytes 3145732
  178.0 29.4 %collective-permute-start.6 = (bf16[1024,512]{0,1:T(8,128)(2,1)S(1)}, bf16[1024,512]{0,1:T(8,128)(2,1)S(1)}, u32[]{:S(2)}, u32[]{:S(2)}) collective-permute-start(bf16[1024,512]{0,1:T(8,128)(2,1)S(1)} %fusion.3), channel_id=1, source_target_pairs={{0,254},{2,0},{4,2},{6,4},{8,6},{10,8},{12,10},{14,12},{16,14},{18... | collective-permute-start | bytes 3145736 | tf_op jit(solution)/shard_map/ppermute | solution.py:12
  197.9 29.4 %collective-permute-start.9 = (bf16[512,1024]{1,0:T(8,128)(2,1)S(1)}, bf16[512,1024]{1,0:T(8,128)(2,1)S(1)}, u32[]{:S(2)}, u32[]{:S(2)}) collective-permute-start(bf16[512,1024]{1,0:T(8,128)(2,1)S(1)} %convolution_convert_fusion), channel_id=1, source_target_pairs={{0,254},{2,0},{4,2},{6,4},{8,6},{10,8},{12,10},{14,12},{16,14},{18... | collective-permute-start | bytes 3145736 | tf_op jit(solution)/shard_map/ppermute | solution.py:12
  208.1 21.8 %collective-permute-start.7 = (bf16[1024,512]{0,1:T(8,128)(2,1)S(1)}, bf16[1024,512]{0,1:T(8,128)(2,1)S(1)}, u32[]{:S(2)}, u32[]{:S(2)}) collective-permute-start(bf16[1024,512]{0,1:T(8,128)(2,1)S(1)} %fusion.2), channel_id=1, source_target_pairs={{0,254},{2,0},{4,2},{6,4},{8,6},{10,8},{12,10},{14,12},{16,14},{18... | collective-permute-start | bytes 3145736 | tf_op jit(solution)/shard_map/ppermute | solution.py:12
  223.6 3.0 copy-start.6
  229.2 76.7 %collective-permute-start.10 = (bf16[512,1024]{1,0:T(8,128)(2,1)}, bf16[512,1024]{1,0:T(8,128)(2,1)}, u32[]{:S(2)}, u32[]{:S(2)}) collective-permute-start(bf16[512,1024]{1,0:T(8,128)(2,1)} %add_convert_fusion.2), channel_id=1, source_target_pairs={{0,254},{2,0},{4,2},{6,4},{8,6},{10,8},{12,10},{14,12},{16,14},{18... | collective-permute-start | bytes 3145736 | tf_op jit(solution)/shard_map/ppermute | solution.py:12
  231.3 89.2 %collective-permute-start.8 = (bf16[1024,512]{0,1:T(8,128)(2,1)}, bf16[1024,512]{0,1:T(8,128)(2,1)}, u32[]{:S(2)}, u32[]{:S(2)}) collective-permute-start(bf16[1024,512]{0,1:T(8,128)(2,1)} %fusion.1), channel_id=1, source_target_pairs={{0,254},{2,0},{4,2},{6,4},{8,6},{10,8},{12,10},{14,12},{16,14},{18... | collective-permute-start | bytes 3145736 | tf_op jit(solution)/shard_map/ppermute | solution.py:12
  309.1 23.7 %collective-permute-start.11 = (bf16[512,1024]{1,0:T(8,128)(2,1)}, bf16[512,1024]{1,0:T(8,128)(2,1)}, u32[]{:S(2)}, u32[]{:S(2)}) collective-permute-start(bf16[512,1024]{1,0:T(8,128)(2,1)} %add_convert_fusion.1), channel_id=1, source_target_pairs={{0,254},{2,0},{4,2},{6,4},{8,6},{10,8},{12,10},{14,12},{16,14},{18... | collective-permute-start | bytes 3145736 | tf_op jit(solution)/shard_map/ppermute | solution.py:12
  323.1 6.6 %copy-start.2 = (f32[448,1024]{1,0:T(8,128)S(1)}, f32[448,1024]{1,0:T(8,128)}, u32[]{:S(2)}) copy-start(f32[448,1024]{1,0:T(8,128)} %fusion.154) | copy-start | bytes 5505028
  323.1 32.0 %all-to-all-start = ((bf16[2,512,512]{1,2,0:T(8,128)(2,1)}), bf16[2,512,512]{1,2,0:T(8,128)(2,1)}, u32[]{:S(2)}, u32[]{:S(2)}) async-start(bf16[2,512,512]{1,2,0:T(8,128)(2,1)} %bitcast.73), calls=%async_computation | async-start | bytes 2097152 | tf_op jit(solution)/shard_map/all_to_all | solution.py:31
  327.6 2.1 copy-start.1
  329.7 3.1 copy-start.3
  334.4 24.3 %copy-start.7 = (bf16[1024,512]{1,0:T(8,128)(2,1)S(1)}, bf16[1024,512]{1,0:T(8,128)(2,1)}, u32[]{:S(2)}) copy-start(bf16[1024,512]{1,0:T(8,128)(2,1)} %copy-done.6) | copy-start | bytes 3145732
  355.1 17.0 %all-to-all-start.1 = ((bf16[2,512,512]{2,1,0:T(8,128)(2,1)}), bf16[2,512,512]{2,1,0:T(8,128)(2,1)S(1)}, u32[]{:S(2)}, u32[]{:S(2)}) async-start(bf16[2,512,512]{2,1,0:T(8,128)(2,1)} %bitcast.71), calls=%async_computation.1 | async-start | bytes 2097152 | tf_op jit(solution)/shard_map/all_to_all | solution.py:31
  (2 other events, 3.3 us)
where the time goes:
time: 374 us; the launch traced here: 373 us
  waiting for transfers between devices  173 us (46%)
  starting transfers between devices  132 us (35%)
  matrix products  53.3 us (14%)
  other arithmetic  10.4 us (3%)
  local copies, waits for them, and re-layouts  3.9 us (1%)
    ppermute x12, waiting for transfers between devices, from_behind(): return lax.ppermute(value, axis, pairs)  152 us
    ppermute x12, starting transfers between devices, from_behind(): return lax.ppermute(value, axis, pairs)  124 us
    dot_general x16, matrix products, inner(): lax.dot_general(left, right, (((left_dim,), (right_dim,)), ((), ())), pre...  29.3 us
    all_to_all x2, waiting for transfers between devices, summed_on_arrival(): lax.all_to_all(tiles, axis, split_axis=0, concat_axis=0, tiled=True)  20.5 us
    dot_general x4, matrix products, on_device(): jnp.dot(jax.nn.gelu(preact).astype(jnp.bfloat16), w_out_slot, preferred_e...  18.4 us
    all_to_all x2, starting transfers between devices, summed_on_arrival(): lax.all_to_all(tiles, axis, split_axis=0, concat_axis=0, tiled=True)  8.11 us
  transfers between devices with their start and end apart: 14, of which 8 were waited for; matrix products, arithmetic and copies ran while one was open for 18% of the time, Pallas kernels for 0%

commit v1 on v0

v1 whole, which is shorter than its diff:
```python
import jax
import jax.numpy as jnp
from jax import lax
from jax.experimental import pallas as pl
from jax.experimental.pallas import tpu as pltpu
from jax.sharding import PartitionSpec as P

MESH = pl.DeviceIdType.MESH
MB, D, HID, CH = 448, 1024, 512, 128
HALF = HID // 2
F32, BF16 = jnp.float32, jnp.bfloat16
SQ = 0.7978845608028654

P1C0, P2C0, P3C0, P1C1, P2C1, P3C1 = range(6)


def inner(left, right, left_dim, right_dim):
    return lax.dot_general(
        left, right, (((left_dim,), (right_dim,)), ((), ())), preferred_element_type=F32
    )


def kernel(
    fwd_hbm, bwd_hbm, cot_hbm, win_hbm, wout_hbm,
    fout, iout, inout, downout,
    tok, w_i, w_o, facc, iacc, orecv, grad, own_send, gs, p1sum, keep, final, g3,
    rly_i, rly_o, rly_b,
    loc_sem, wx_send, wx_recv, tok_send, tok_recv,
    xp_send, xp_recv, rf_send, rf_recv,
    own_sem, fin_sem, xm_send, g3_sem, rb_send, rb_recv, out_send, out_recv,
):
    blk, rep = lax.axis_index("blk"), lax.axis_index("rep")
    core = lax.rem(blk, 2)
    chip = lax.div(blk, 2)
    pos = lax.rem(chip, 16)
    zhi = lax.div(chip, 16)
    other, orep = 1 - core, 1 - rep

    def at(chip_, core_, rep_):
        return (lax.rem(chip_ + 64, 64) * 2 + core_, rep_)

    def corner(p):
        return pos == p

    def in_plane(p, core_=core):
        return at(zhi * 16 + p, core_, rep)

    def remote(src, dst, ssem, rsem, dev):
        return pltpu.make_async_remote_copy(
            src_ref=src, dst_ref=dst, send_sem=ssem, recv_sem=rsem,
            device_id=dev, device_id_type=MESH,
        )

    peer = at(chip, other, rep)
    ahead = at(chip + 1, core, rep)
    SRC_F, SRC_B = 15, 0

    def local_w(q):
        cols = pl.ds(pl.multiple_of(core * HALF + q * CH, CH), CH)
        return (
            pltpu.make_async_copy(win_hbm.at[:, cols], w_i.at[2 * core + q], loc_sem.at[3 + q]),
            pltpu.make_async_copy(wout_hbm.at[cols, :], w_o.at[2 * core + q], loc_sem.at[5 + q]),
        )

    toks = (fwd_hbm, bwd_hbm, cot_hbm)
    local_t = [pltpu.make_async_copy(toks[t], tok.at[t, core], loc_sem.at[t]) for t in range(3)]
    for q in range(2):
        for copy in local_w(q):
            copy.start()
    for copy in local_t:
        copy.start()

    barrier = pltpu.get_barrier_semaphore()

    def greet(dev):
        pl.semaphore_signal(barrier, inc=1, device_id=dev, device_id_type=MESH)

    greet(peer)
    for core_ in range(2):
        greet(at(chip, core_, orep))
        for rep_ in range(2):
            greet(at(chip + 1, core_, rep_))
            greet(at(chip - 1, core_, rep_))
    for p in (0, 3, 12, 15):
        @pl.when(corner(p))
        def _():
            for other_p in (0, 3, 12, 15):
                if other_p != p:
                    greet(in_plane(other_p))
    is_corner = corner(0) | corner(3) | corner(12) | corner(15)

    @pl.when(jnp.logical_not(is_corner))
    def _():
        pl.semaphore_wait(barrier, 11)

    @pl.when(is_corner)
    def _():
        pl.semaphore_wait(barrier, 14)

    def swap_w(q):
        cols = pl.ds(pl.multiple_of(other * HALF + q * CH, CH), CH)
        return (
            remote(win_hbm.at[:, cols], w_i.at[2 * core + q], wx_send.at[q, 0], wx_recv.at[q, 0], peer),
            remote(wout_hbm.at[cols, :], w_o.at[2 * core + q], wx_send.at[q, 1], wx_recv.at[q, 1], peer),
        )

    swaps = [copy for q in range(2) for copy in swap_w(q)]
    for copy in swaps:
        copy.start()
    swap_t = [
        remote(toks[t], tok.at[t, core], tok_send.at[t], tok_recv.at[t], peer) for t in range(3)
    ]
    for copy in swap_t:
        copy.start()

    def arrived_w(q):
        return (
            pltpu.make_async_remote_copy(
                src_ref=w_i.at[2 * other + q], dst_ref=w_i.at[2 * other + q],
                send_sem=wx_send.at[q, 0], recv_sem=wx_recv.at[q, 0],
                device_id=peer, device_id_type=MESH),
            pltpu.make_async_remote_copy(
                src_ref=w_o.at[2 * other + q], dst_ref=w_o.at[2 * other + q],
                send_sem=wx_send.at[q, 1], recv_sem=wx_recv.at[q, 1],
                device_id=peer, device_id_type=MESH),
        )

    def piece_w(ref_i, ref_o, n, s):
        if s < 2:
            return ref_i.at[n, pl.ds(s * 512, 512)]
        return ref_o.at[n, pl.ds((s - 2) * 64, 64)]

    RELAY_F = {1: 0, 2: 12, 3: 3}
    RELAY_B = {1: 15, 2: 3, 3: 12}

    def rly_w(i, s):
        return rly_i.at[i] if s == 1 else rly_o.at[i]

    def whole_w(i, n):
        return (
            remote(w_i.at[n], w_i.at[4 + i], xp_send.at[i, 0], xp_recv.at[i, 0], ahead),
            remote(w_o.at[n], w_o.at[4 + i], xp_send.at[i, 1], xp_recv.at[i, 1], ahead),
        )

    def send_w(i, n):
        @pl.when(jnp.logical_not(corner(SRC_F)))
        def _():
            for copy in whole_w(i, n):
                copy.start()

        @pl.when(corner(SRC_F))
        def _():
            for s in (1, 2, 3):
                remote(piece_w(w_i, w_o, n, s), rly_w(i, s), xp_send.at[i, s // 2], rf_recv.at[i],
                       in_plane(RELAY_F[s])).start()
            remote(piece_w(w_i, w_o, n, 0), piece_w(w_i, w_o, 4 + i, 0), xp_send.at[i, 0],
                   xp_recv.at[i, 0], ahead).start()

    def pass_w(i):
        dev = at((zhi + 1) * 16, core, rep)
        for s, p in RELAY_F.items():
            @pl.when(corner(p))
            def _():
                copy = remote(rly_w(i, s), piece_w(w_i, w_o, 4 + i, s), rf_send.at[i],
                              xp_recv.at[i, s // 2], dev)
                remote(rly_w(i, s), rly_w(i, s), rf_send.at[i], rf_recv.at[i], dev).wait_recv()
                copy.start()

    def passed_w(i):
        for s, p in RELAY_F.items():
            @pl.when(corner(p))
            def _():
                remote(rly_w(i, s), rly_w(i, s), rf_send.at[i], rf_recv.at[i], ahead).wait_send()

    def place_g(i, h):
        q, kind = i // 3, i % 3 + 1
        if kind == 3:
            return g3.at[q, h], g3_sem.at[q], core, rep
        return final.at[1, rep, core, q], fin_sem.at[1, rep, core, q], 2 - kind, h

    def piece_g(ref, s):
        return ref.at[s // 2, pl.ds((s % 2) * 64, 64)]

    def send_g(i):
        for h in range(2):
            dst, sem, core_, rep_ = place_g(i, h)
            dev = at(chip - 1, core_, rep_)

            @pl.when(jnp.logical_not(corner(SRC_B)))
            def _():
                remote(gs.at[i, h], dst, xm_send.at[i, h], sem, dev).start()

            @pl.when(corner(SRC_B))
            def _():
                for s in (1, 2, 3):
                    remote(piece_g(gs.at[i, h], s), rly_b.at[i, h], xm_send.at[i, h],
                           rb_recv.at[i, h], in_plane(RELAY_B[s])).start()
                remote(piece_g(gs.at[i, h], 0), piece_g(dst, 0), xm_send.at[i, h], sem, dev).start()

    def pass_g(i):
        for s, p in RELAY_B.items():
            @pl.when(corner(p))
            def _():
                for h in range(2):
                    dst, sem, core_, rep_ = place_g(i, h)
                    dev = at(zhi * 16 - 1, core_, rep_)
                    copy = remote(rly_b.at[i, h], piece_g(dst, s), rb_send.at[i, h], sem, dev)
                    remote(rly_b.at[i, h], rly_b.at[i, h], rb_send.at[i, h], rb_recv.at[i, h],
                           dev).wait_recv()
                    copy.start()

    def passed_g(i):
        for s, p in RELAY_B.items():
            @pl.when(corner(p))
            def _():
                for h in range(2):
                    remote(rly_b.at[i, h], rly_b.at[i, h], rb_send.at[i, h], rb_recv.at[i, h],
                           ahead).wait_send()

    def compute(n, lo, hi):
        grad[...] = jnp.zeros_like(grad)

        def block(b, carry):
            wi, wo = w_i[n], w_o[n]
            pre = jnp.dot(tok[0, b], wi, preferred_element_type=F32)
            hid = (0.5 * pre * (1.0 + jnp.tanh(SQ * (pre + 0.044715 * (pre * pre * pre))))).astype(BF16)
            facc[b] += jnp.dot(hid, wo, preferred_element_type=F32)
            pre = jnp.dot(tok[1, b], wi, preferred_element_type=F32)
            hid_grad = inner(tok[2, b], wo, 1, 1)
            square = pre * pre
            t = jnp.tanh(SQ * (pre + 0.044715 * (square * pre)))
            cdf = 0.5 * (1.0 + t)
            slope = cdf + pre * (0.5 * (1.0 - t * t)) * (SQ * (1.0 + 3 * 0.044715 * square))
            hid = (pre * cdf).astype(BF16)
            pre_grad = (hid_grad * slope).astype(BF16)
            iacc[b] += inner(pre_grad, wi, 1, 1)
            grad[0] += inner(pre_grad, tok[1, b], 0, 0)
            grad[1] += inner(hid, tok[2, b], 0, 0)
            return carry

        lax.fori_loop(lo, hi, block, 0)

    def halves(ref, h):
        return ref[:, :, pl.ds(h * 512, 512)]

    for q in range(2):
        for copy in local_w(q):
            copy.wait()
        for copy in arrived_w(q):
            copy.wait_recv()
        if q == 0:
            send_w(P1C0, 2)
            send_w(P2C0, 0)
    facc[...] = jnp.zeros_like(facc)
    iacc[...] = jnp.zeros_like(iacc)
    for t in range(3):
        local_t[t].wait()
    for t in range(3):
        remote(toks[t], tok.at[t, other], tok_send.at[t], tok_recv.at[t], peer).wait_recv()

    def own_copy(n, h):
        j, q = lax.div(n, 2), lax.rem(n, 2)
        return remote(own_send.at[n, h], final.at[0, rep, core, q], own_sem.at[n, h],
                      fin_sem.at[0, rep, core, q], at(chip, j, h))

    def own_step(n, carry):
        j, q = lax.div(n, 2), lax.rem(n, 2)
        compute(n, j, 2)
        for h in range(2):
            mine = (core == j) & (rep == h)

            @pl.when(mine)
            def _():
                keep[q] = halves(grad, h)

            @pl.when(jnp.logical_not(mine))
            def _():
                own_send[n, h] = halves(grad, h).astype(BF16)
                own_copy(n, h).start()
        return carry

    lax.fori_loop(0, 4, own_step, 0)

    def finish_p1(q):
        for h in range(2):
            if h == 0:
                remote(g3.at[q], g3.at[q], xm_send.at[0, 0], g3_sem.at[q], ahead).wait_recv()
            gs[3 * q, h] = (halves(p1sum.at[q], h) + g3[q, h].astype(F32)).astype(BF16)
        send_g(3 * q)

    for i in range(6):
        q, kind = i // 3, i % 3 + 1
        pass_w(i)
        for copy in whole_w(i, 4 + i):
            copy.wait_recv()
        if kind == 1:
            send_w(3 * q + 2, 4 + i)
            if q == 0:
                send_w(P1C1, 3)
                send_w(P2C1, 1)
        compute(4 + i, 0, 1 if kind == 3 else 2)
        if kind == 1:
            p1sum[q] = grad[...]
        else:
            for h in range(2):
                gs[i, h] = halves(grad, h).astype(BF16)
            send_g(i)
        if i == 2:
            pass_g(P2C0)
        if i == 3:
            pass_g(P3C0)
            finish_p1(0)
        if i == 4:
            pass_g(P1C0)

    outs = [
        remote(acc.at[other], orecv.at[a], out_send.at[a], out_recv.at[a], peer)
        for a, acc in enumerate((facc, iacc))
    ]
    for copy in outs:
        copy.start()
    pass_g(P2C1)
    pass_g(P3C1)
    finish_p1(1)

    for a, (acc, out) in enumerate(((facc, fout), (iacc, iout))):
        outs[a].wait_recv()
        out[...] = (acc[core] + orecv[a]).astype(BF16)

    def arrived(side, rep_, core_, q):
        ref = final.at[side, rep_, core_, q]
        remote(ref, ref, xm_send.at[0, 0], fin_sem.at[side, rep_, core_, q], ahead).wait_recv()
        return ref[...].astype(F32)

    def finish(q):
        for core_ in (core, other):
            total = keep[q] if core_ is core else arrived(0, rep, core_, q)
            total = total + arrived(0, orep, core_, q)
            total = total + arrived(1, rep, core_, q)
            total = total + arrived(1, orep, core_, q)
            at_hid = pl.multiple_of(core_ * HALF + q * CH, CH)
            inout[:, pl.ds(at_hid, CH)] = total[0].T
            downout[pl.ds(at_hid, CH), :] = total[1]

    finish(0)
    pass_g(P1C1)
    finish(1)

    for copy in swaps + swap_t + outs:
        copy.wait_send()
    for i in range(6):
        for copy in whole_w(i, 4 + i):
            copy.wait_send()
        passed_w(i)
        passed_g(i)
        for h in range(2):
            remote(gs.at[i, h], gs.at[i, h], xm_send.at[i, h], g3_sem.at[0], ahead).wait_send()
    for n in range(4):
        for h in range(2):
            @pl.when(jnp.logical_not((core == n // 2) & (rep == h)))
            def _():
                own_copy(n, h).wait_send()


def on_device(fwd_in, bwd_in, cotangent, w_in, w_out):
    dma = pltpu.SemaphoreType.DMA
    vmem = pltpu.VMEM
    return pl.pallas_call(
        kernel,
        out_shape=(
            jax.ShapeDtypeStruct((MB, D), BF16),
            jax.ShapeDtypeStruct((MB, D), BF16),
            jax.ShapeDtypeStruct((HID, HID), F32),
            jax.ShapeDtypeStruct((HID, HID), F32),
        ),
        in_specs=[pl.BlockSpec(memory_space=pl.ANY)] * 5,
        out_specs=[pl.BlockSpec(memory_space=pltpu.VMEM)] * 4,
        scratch_shapes=[
            vmem((3, 2, MB, D), BF16),
            vmem((10, D, CH), BF16),
            vmem((10, CH, D), BF16),
            vmem((2, MB, D), F32),
            vmem((2, MB, D), F32),
            vmem((2, MB, D), F32),
            vmem((2, CH, D), F32),
            vmem((4, 2, 2, CH, 512), BF16),
            vmem((6, 2, 2, CH, 512), BF16),
            vmem((2, 2, CH, D), F32),
            vmem((2, 2, CH, 512), F32),
            vmem((2, 2, 2, 2, 2, CH, 512), BF16),
            vmem((2, 2, 2, CH, 512), BF16),
            vmem((6, 512, CH), BF16),
            vmem((6, 64, D), BF16),
            vmem((6, 2, 64, 512), BF16),
            dma((7,)),
            dma((2, 2)),
            dma((2, 2)),
            dma((3,)),
            dma((3,)),
            dma((6, 2)),
            dma((6, 2)),
            dma((6,)),
            dma((6,)),
            dma((4, 2)),
            dma((2, 2, 2, 2)),
            dma((6, 2)),
            dma((2,)),
            dma((6, 2)),
            dma((6, 2)),
            dma((2,)),
            dma((2,)),
        ],
        compiler_params=pltpu.CompilerParams(
            collective_id=0, has_side_effects=True, vmem_limit_bytes=60 * 2**20
        ),
        cost_estimate=pl.CostEstimate(
            flops=13_153_337_344, bytes_accessed=12 * 2**20, transcendentals=2 * 4 * MB * HID
        ),
    )(fwd_in, bwd_in, cotangent, w_in, w_out)


def solution(mesh):
    in_specs = (
        P(("blk", "rep"), None),
        P(("blk", "rep"), None),
        P(("blk", "rep"), None),
        P(None, "blk"),
        P("blk", None),
    )
    out_specs = (P(("blk", "rep"), None), P(("blk", "rep"), None), P("rep", "blk"), P("blk", "rep"))
    return jax.shard_map(
        on_device, mesh=mesh, in_specs=in_specs, out_specs=out_specs, check_vma=False
    )
```

time: 374 us -> 148 us (0.40)
  the two profiles are of different devices: /device:TPU:64 before, /device:TPU:31 now
where the time goes in v1:
time: 148 us
  Pallas kernels  141 us (95%)
  local copies, waits for them, and re-layouts  6.37 us (4%)
    pallas_call x1, Pallas kernels, on_device(): pl.pallas_call(kernel, out_shape=(jax.ShapeDtypeStruct((MB, D), BF16), ja...  141 us
    unnamed x10, local copies, waits for them, and re-layouts  6.37 us

profile of v1, /device:TPU:31, one launch (start us, length us, event | category | flops | bytes accessed | tf_op | source)
XLA Modules:
  0.0 148.0 jit_solution(12140057354570552068)
XLA Ops:
  0.6 141.0 %shard_map.84 = (bf16[448,1024]{1,0:T(8,128)(2,1)}, bf16[448,1024]{1,0:T(8,128)(2,1)}, f32[512,512]{1,0:T(8,128)}, f32[512,512]{1,0:T(8,128)}) custom-call(bf16[448,1024]{1,0:T(8,128)(2,1)} %fwd_hbm.1, bf16[448,1024]{1,0:T(8,128)(2,1)} %bwd_hbm.1, bf16[448,1024]{1,0:T(8,128)(2,1)} %cot_hbm.1, bf16[1024,512]{1,0:T(8,128)(2,1)} %win_hbm.1, ...), custom_call_target="tpu_custom_call" | custom-call | flops 13153337344 | bytes 12582912 | tf_op jit(solution)/shard_map/pallas_call | solution.py:368
  141.6 0.0 copy-start.2
  141.6 2.2 %copy.13 = bf16[448,1024]{1,0:T(8,128)(2,1)} copy(bf16[448,1024]{1,0:T(8,128)(2,1)} %get-tuple-element.8) | data formatting | bytes 1835008
  143.9 0.0 copy-done.2
  143.9 0.0 copy-start.1
  143.9 0.9 copy.14
  144.8 0.6 copy-done.1
  145.4 0.0 copy-start
  145.4 1.0 copy.15
  146.4 0.6 copy-done
  147.1 1.0 copy.16
Async XLA Ops:
  141.6 2.3 %copy-start.2 = (bf16[448,1024]{1,0:T(8,128)(2,1)S(1)}, bf16[448,1024]{1,0:T(8,128)(2,1)}, u32[]{:S(2)}) copy-start(bf16[448,1024]{1,0:T(8,128)(2,1)} %get-tuple-element.9) | copy-start | bytes 2752516
  143.9 1.6 %copy-start.1 = (f32[512,512]{1,0:T(8,128)S(1)}, f32[512,512]{1,0:T(8,128)}, u32[]{:S(2)}) copy-start(f32[512,512]{1,0:T(8,128)} %get-tuple-element.10) | copy-start | bytes 3145732
  145.4 1.6 %copy-start = (f32[512,512]{1,0:T(8,128)S(1)}, f32[512,512]{1,0:T(8,128)}, u32[]{:S(2)}) copy-start(f32[512,512]{1,0:T(8,128)} %get-tuple-element.11) | copy-start | bytes 3145732

commit v2 on v1

v2 whole, which is shorter than its diff:
```python
import jax
import jax.numpy as jnp
from jax import lax
from jax.experimental import pallas as pl
from jax.experimental.pallas import tpu as pltpu
from jax.sharding import PartitionSpec as P

MESH = pl.DeviceIdType.MESH
MB, D, HID, CH = 448, 1024, 512, 128
HALF = HID // 2
F32, BF16 = jnp.float32, jnp.bfloat16
SQ = 0.7978845608028654

P1C0, P1C1, P3C0, P2C0, P3C1, P2C1 = range(6)
KIND, CHUNK = (1, 1, 3, 2, 3, 2), (0, 1, 0, 0, 1, 1)


def inner(left, right, left_dim, right_dim):
    return lax.dot_general(
        left, right, (((left_dim,), (right_dim,)), ((), ())), preferred_element_type=F32
    )


def kernel(
    fwd_hbm, bwd_hbm, cot_hbm, win_hbm, wout_hbm,
    fout, iout, inout, downout,
    tok, w_i, w_o, facc, iacc, orecv, grad, own_send, gs, hold, zs, zr, keep, final, g3,
    p1full, ownfull, lrecv,
    rly_i, rly_o, rly_b,
    loc_sem, wx_send, wx_recv, tok_send, tok_recv,
    xp_send, xp_recv, xd_send, rf_send, rf_recv,
    own_sem, fin_sem, xm_send, g3_sem, z_send, z_recv, rb_send, rb_recv, out_send, out_recv, l_sem,
):
    blk, rep = lax.axis_index("blk"), lax.axis_index("rep")
    core = lax.rem(blk, 2)
    chip = lax.div(blk, 2)
    pos = lax.rem(chip, 16)
    zhi = lax.div(chip, 16)
    other, orep = 1 - core, 1 - rep

    def at(chip_, core_, rep_):
        return (lax.rem(chip_ + 64, 64) * 2 + core_, rep_)

    def corner(p):
        return pos == p

    def in_plane(p, core_=core):
        return at(zhi * 16 + p, core_, rep)

    def remote(src, dst, ssem, rsem, dev):
        return pltpu.make_async_remote_copy(
            src_ref=src, dst_ref=dst, send_sem=ssem, recv_sem=rsem,
            device_id=dev, device_id_type=MESH,
        )

    peer = at(chip, other, rep)
    ahead = at(chip + 1, core, rep)
    SRC_F, SRC_B = 15, 0

    def local_w(q):
        cols = pl.ds(pl.multiple_of(core * HALF + q * CH, CH), CH)
        return (
            pltpu.make_async_copy(win_hbm.at[:, cols], w_i.at[2 * core + q], loc_sem.at[3 + q]),
            pltpu.make_async_copy(wout_hbm.at[cols, :], w_o.at[2 * core + q], loc_sem.at[5 + q]),
        )

    toks = (fwd_hbm, bwd_hbm, cot_hbm)
    local_t = [pltpu.make_async_copy(toks[t], tok.at[t, core], loc_sem.at[t]) for t in range(3)]
    for q in range(2):
        for copy in local_w(q):
            copy.start()
    for copy in local_t:
        copy.start()

    barrier = pltpu.get_barrier_semaphore()

    def greet(dev):
        pl.semaphore_signal(barrier, inc=1, device_id=dev, device_id_type=MESH)

    greet(peer)
    for core_ in range(2):
        greet(at(chip, core_, orep))
        for rep_ in range(2):
            greet(at(chip + 1, core_, rep_))
            greet(at(chip - 1, core_, rep_))
    for p in (0, 3, 12, 15):
        @pl.when(corner(p))
        def _():
            for other_p in (0, 3, 12, 15):
                if other_p != p:
                    greet(in_plane(other_p))
    is_corner = corner(0) | corner(3) | corner(12) | corner(15)

    @pl.when(jnp.logical_not(is_corner))
    def _():
        pl.semaphore_wait(barrier, 11)

    @pl.when(is_corner)
    def _():
        pl.semaphore_wait(barrier, 14)

    def swap_w(q):
        cols = pl.ds(pl.multiple_of(other * HALF + q * CH, CH), CH)
        return (
            remote(win_hbm.at[:, cols], w_i.at[2 * core + q], wx_send.at[q, 0], wx_recv.at[q, 0], peer),
            remote(wout_hbm.at[cols, :], w_o.at[2 * core + q], wx_send.at[q, 1], wx_recv.at[q, 1], peer),
        )

    swaps = [copy for q in range(2) for copy in swap_w(q)]
    for copy in swaps:
        copy.start()
    swap_t = [
        remote(toks[t], tok.at[t, core], tok_send.at[t], tok_recv.at[t], peer) for t in range(3)
    ]
    for copy in swap_t:
        copy.start()

    def arrived_w(q):
        return (
            pltpu.make_async_remote_copy(
                src_ref=w_i.at[2 * other + q], dst_ref=w_i.at[2 * other + q],
                send_sem=wx_send.at[q, 0], recv_sem=wx_recv.at[q, 0],
                device_id=peer, device_id_type=MESH),
            pltpu.make_async_remote_copy(
                src_ref=w_o.at[2 * other + q], dst_ref=w_o.at[2 * other + q],
                send_sem=wx_send.at[q, 1], recv_sem=wx_recv.at[q, 1],
                device_id=peer, device_id_type=MESH),
        )

    STREAM_F = {0: (None, (0, 768), None), 1: (0, (768, 256), (0, 32)), 2: (12, None, (32, 64)),
                3: (3, None, (96, 32))}
    STREAM_B = {0: (None, 0, 0), 1: (15, 0, 64), 2: (3, 1, 0), 3: (12, 1, 64)}

    def pieces_w(n, s):
        _, rows_i, rows_o = STREAM_F[s]
        out = []
        for a, (ref, rows) in enumerate(((w_i, rows_i), (w_o, rows_o))):
            if rows is not None:
                out.append((a, ref.at[n, pl.ds(*rows)], (rly_i, rly_o)[a], rows[1]))
        return out

    def whole_w(i, n):
        return (
            remote(w_i.at[n], w_i.at[4 + i], xp_send.at[i, 0], xp_recv.at[i, 0], ahead),
            remote(w_o.at[n], w_o.at[4 + i], xp_send.at[i, 1], xp_recv.at[i, 1], ahead),
        )

    first_ahead = at(chip + 1, core, 0)
    sends_f = corner(SRC_F) & (rep == 1)

    def direct_w(i, n):
        _, src, _, _ = pieces_w(n, 0)[0]
        _, dst, _, _ = pieces_w(4 + i, 0)[0]
        return (remote(src, dst, xp_send.at[i, 0], xp_recv.at[i, 0], ahead),
                remote(src, dst, xd_send.at[i], xp_recv.at[i, 0], first_ahead))

    def send_w(i, n):
        @pl.when(jnp.logical_not(corner(SRC_F)))
        def _():
            for copy in whole_w(i, n):
                copy.start()

        @pl.when(sends_f)
        def _():
            for s in (1, 2, 3):
                for a, src, rly, size in pieces_w(n, s):
                    remote(src, rly.at[i, pl.ds(0, size)], xp_send.at[i, a], rf_recv.at[i, a],
                           in_plane(STREAM_F[s][0])).start()
            for copy in direct_w(i, n):
                copy.start()

    def sent_w(i):
        @pl.when(jnp.logical_not(corner(SRC_F)) | sends_f)
        def _():
            for copy in whole_w(i, 4 + i):
                copy.wait_send()

        @pl.when(sends_f)
        def _():
            direct_w(i, 4 + i)[1].wait_send()

    def relays_w(i):
        for s, (via, _, _) in STREAM_F.items():
            if via is not None:
                copies = []
                for a, dst, rly, size in pieces_w(4 + i, s):
                    held = rly.at[i, pl.ds(0, size)]
                    devs = [at((zhi + 1) * 16, core, rep_) for rep_ in range(2)]
                    copies.append((
                        remote(held, held, rf_send.at[i, a, 0], rf_recv.at[i, a], devs[0]),
                        [remote(held, dst, rf_send.at[i, a, rep_], xp_recv.at[i, a], devs[rep_])
                         for rep_ in (1, 0)],
                    ))
                yield via, copies

    def pass_w(i):
        for via, copies in relays_w(i):
            @pl.when(corner(via) & (rep == 1))
            def _():
                for come, gone in copies:
                    come.wait_recv()
                    for go in gone:
                        go.start()

    def passed_w(i):
        for via, copies in relays_w(i):
            @pl.when(corner(via) & (rep == 1))
            def _():
                for come, gone in copies:
                    for go in gone:
                        go.wait_send()

    def parts_g(i):
        q, kind = CHUNK[i], KIND[i]
        if q == 1:
            if kind == 3:
                return [(8, g3.at[2], g3_sem.at[1], core)]
            return [(5 + kind, final.at[2, core, 1], fin_sem.at[2, core, 1], 2 - kind)]
        if kind == 3:
            return [(4 + h, g3.at[h], g3_sem.at[0], core) for h in range(2)]
        return [(2 * kind - 2 + h, lrecv.at[2 - kind, h], l_sem.at[2 - kind], core) for h in range(2)]

    def piece_g(ref, s):
        _, a, row = STREAM_B[s]
        return ref.at[a, pl.ds(row, 64)]

    def send_g(i):
        for slot, dst, sem, core_ in parts_g(i):
            dev = at(chip - 1, core_, rep)

            @pl.when(jnp.logical_not(corner(SRC_B)))
            def _():
                remote(gs.at[slot], dst, xm_send.at[slot], sem, dev).start()

            @pl.when(corner(SRC_B))
            def _():
                for s in (1, 2, 3, 0):
                    via = STREAM_B[s][0]
                    if via is None:
                        remote(piece_g(gs.at[slot], s), piece_g(dst, s), xm_send.at[slot], sem,
                               dev).start()
                    else:
                        remote(piece_g(gs.at[slot], s), rly_b.at[slot], xm_send.at[slot],
                               rb_recv.at[slot], in_plane(via)).start()

    def relays_g(i):
        for slot, dst, sem, core_ in parts_g(i):
            dev = at(zhi * 16 - 1, core_, rep)
            for s, (via, _, _) in STREAM_B.items():
                if via is not None:
                    yield via, (
                        remote(rly_b.at[slot], rly_b.at[slot], rb_send.at[slot], rb_recv.at[slot], dev),
                        remote(rly_b.at[slot], piece_g(dst, s), rb_send.at[slot], sem, dev),
                    )

    def pass_g(i):
        for via, (come, go) in relays_g(i):
            @pl.when(corner(via))
            def _():
                come.wait_recv()
                go.start()

    def passed_g(i):
        for via, (come, go) in relays_g(i):
            @pl.when(corner(via))
            def _():
                go.wait_send()

    def compute(n, lo, hi):
        grad[...] = jnp.zeros_like(grad)

        def block(b, carry):
            wi, wo = w_i[n], w_o[n]
            pre = jnp.dot(tok[0, b], wi, preferred_element_type=F32)
            hid = (0.5 * pre * (1.0 + jnp.tanh(SQ * (pre + 0.044715 * (pre * pre * pre))))).astype(BF16)
            facc[b] += jnp.dot(hid, wo, preferred_element_type=F32)
            pre = jnp.dot(tok[1, b], wi, preferred_element_type=F32)
            hid_grad = inner(tok[2, b], wo, 1, 1)
            square = pre * pre
            t = jnp.tanh(SQ * (pre + 0.044715 * (square * pre)))
            cdf = 0.5 * (1.0 + t)
            slope = cdf + pre * (0.5 * (1.0 - t * t)) * (SQ * (1.0 + 3 * 0.044715 * square))
            hid = (pre * cdf).astype(BF16)
            pre_grad = (hid_grad * slope).astype(BF16)
            iacc[b] += inner(pre_grad, wi, 1, 1)
            grad[0] += inner(pre_grad, tok[1, b], 0, 0)
            grad[1] += inner(hid, tok[2, b], 0, 0)
            return carry

        lax.fori_loop(lo, hi, block, 0)

    def halves(ref, h):
        return ref[:, :, pl.ds(h * 512, 512)]

    for q in range(2):
        for copy in local_w(q):
            copy.wait()
        for copy in arrived_w(q):
            copy.wait_recv()
        send_w(P1C0 + q, 2 + q)
    facc[...] = jnp.zeros_like(facc)
    iacc[...] = jnp.zeros_like(iacc)
    for t in range(3):
        local_t[t].wait()
    for t in range(3):
        remote(toks[t], tok.at[t, other], tok_send.at[t], tok_recv.at[t], peer).wait_recv()

    def own_copy(n, h):
        j, q = n // 2, n % 2
        return remote(own_send.at[n, h], final.at[rep, core, q], own_sem.at[n, h],
                      fin_sem.at[rep, core, q], at(chip, j, h))

    def hand_out(n, h, value):
        mine = (core == n // 2) & (rep == h)

        @pl.when(mine)
        def _():
            keep[n % 2] = value

        @pl.when(jnp.logical_not(mine))
        def _():
            own_send[n, h] = value.astype(BF16)
            own_copy(n, h).start()

    for n in (1, 3):
        compute(n, n // 2, 2)
        for h in range(2):
            hand_out(n, h, halves(grad, h))
    pass_w(P1C0)

    def own_step(j, carry):
        compute(2 * j, j, 2)
        ownfull[j] = grad[...]
        return carry

    lax.fori_loop(0, 2, own_step, 0)
    pass_w(P1C1)

    def merge_own(j):
        remote(lrecv.at[j], lrecv.at[j], z_send.at[0], l_sem.at[j], ahead).wait_recv()
        for h in range(2):
            hand_out(2 * j, h, halves(ownfull.at[j], h) + lrecv[j, h].astype(F32))

    def my_half(ref, h):
        return ref[:, :, pl.ds(pl.multiple_of(h * 512, 512), 512)]

    orep_dev = at(chip, core, orep)

    def swap_z(i):
        return remote(zs.at[i], zr.at[i], z_send.at[i], z_recv.at[i], orep_dev)

    def finish_z(i):
        swap_z(i).wait_recv()
        total = hold[i] + zr[i].astype(F32)
        if KIND[i] == 1:
            hold[i] = total
        else:
            gs[parts_g(i)[0][0]] = total.astype(BF16)
            send_g(i)

    def send_whole(i, more=False):
        for h, (slot, _, _, _) in enumerate(parts_g(i)):
            if more:
                gs[slot] = (halves(p1full, h) + g3[h].astype(F32)).astype(BF16)
            else:
                gs[slot] = halves(grad, h).astype(BF16)
        send_g(i)

    def finish_p1(q):
        if q == 0:
            both = g3.at[pl.ds(0, 2)]
            remote(both, both, z_send.at[0], g3_sem.at[0], ahead).wait_recv()
            send_whole(P1C0, True)
        else:
            remote(g3.at[2], g3.at[2], z_send.at[0], g3_sem.at[1], ahead).wait_recv()
            gs[parts_g(P1C1)[0][0]] = (hold[P1C1] + g3[2].astype(F32)).astype(BF16)
            send_g(P1C1)

    for i in range(6):
        q, kind = CHUNK[i], KIND[i]
        for early in ((), (P3C0,), (P2C0,), (P3C1, P2C1), (), ())[i]:
            pass_w(early)
        if i == 2:
            finish_z(P1C1)
        if i == 4:
            pass_g(P3C0)
            finish_p1(0)
        if i == 5:
            finish_z(P3C1)
            pass_g(P2C0)
        for copy in whole_w(i, 4 + i):
            copy.wait_recv()
        if i == 0:
            send_w(P3C0, 4 + i)
        if i == 1:
            send_w(P2C0, 0)
            send_w(P3C1, 4 + i)
            send_w(P2C1, 1)
        compute(4 + i, 0, 1 if kind == 3 else 2)
        if i == P1C0:
            p1full[...] = grad[...]
        elif q == 0:
            send_whole(i)
        else:
            hold[i] = my_half(grad, rep)
            zs[i] = my_half(grad, orep).astype(BF16)
            swap_z(i).start()

    outs = [
        remote(acc.at[other], orecv.at[a], out_send.at[a], out_recv.at[a], peer)
        for a, acc in enumerate((facc, iacc))
    ]
    for copy in outs:
        copy.start()
    pass_g(P1C0)
    merge_own(0)
    finish_z(P2C1)
    pass_g(P3C1)
    finish_p1(1)
    merge_own(1)
    pass_g(P2C1)
    pass_g(P1C1)

    for a, (acc, out) in enumerate(((facc, fout), (iacc, iout))):
        outs[a].wait_recv()
        out[...] = (acc[core] + orecv[a]).astype(BF16)

    def arrived(slot, core_, q):
        ref = final.at[slot, core_, q]
        remote(ref, ref, z_send.at[0], fin_sem.at[slot, core_, q], ahead).wait_recv()
        return ref[...].astype(F32)

    def finish(q):
        for core_ in (core, other):
            total = keep[q] if core_ is core else arrived(rep, core_, q)
            total = total + arrived(orep, core_, q)
            if q == 1:
                total = total + arrived(2, core_, q)
            at_hid = pl.multiple_of(core_ * HALF + q * CH, CH)
            inout[:, pl.ds(at_hid, CH)] = total[0].T
            downout[pl.ds(at_hid, CH), :] = total[1]

    finish(0)
    finish(1)

    for copy in swaps + swap_t + outs:
        copy.wait_send()
    for i in range(6):
        sent_w(i)
        passed_w(i)
        passed_g(i)
        for slot, _, _, _ in parts_g(i):
            remote(gs.at[slot], gs.at[slot], xm_send.at[slot], g3_sem.at[0], ahead).wait_send()
        if CHUNK[i] == 1:
            swap_z(i).wait_send()
    for n in range(4):
        for h in range(2):
            @pl.when(jnp.logical_not((core == n // 2) & (rep == h)))
            def _():
                own_copy(n, h).wait_send()


def on_device(fwd_in, bwd_in, cotangent, w_in, w_out):
    dma = pltpu.SemaphoreType.DMA
    vmem = pltpu.VMEM
    return pl.pallas_call(
        kernel,
        out_shape=(
            jax.ShapeDtypeStruct((MB, D), BF16),
            jax.ShapeDtypeStruct((MB, D), BF16),
            jax.ShapeDtypeStruct((HID, HID), F32),
            jax.ShapeDtypeStruct((HID, HID), F32),
        ),
        in_specs=[pl.BlockSpec(memory_space=pl.ANY)] * 5,
        out_specs=[pl.BlockSpec(memory_space=pltpu.VMEM)] * 4,
        scratch_shapes=[
            vmem((3, 2, MB, D), BF16),
            vmem((10, D, CH), BF16),
            vmem((10, CH, D), BF16),
            vmem((2, MB, D), F32),
            vmem((2, MB, D), F32),
            vmem((2, MB, D), F32),
            vmem((2, CH, D), F32),
            vmem((4, 2, 2, CH, 512), BF16),
            vmem((9, 2, CH, 512), BF16),
            vmem((6, 2, CH, 512), F32),
            vmem((6, 2, CH, 512), BF16),
            vmem((6, 2, CH, 512), BF16),
            vmem((2, 2, CH, 512), F32),
            vmem((3, 2, 2, 2, CH, 512), BF16),
            vmem((3, 2, CH, 512), BF16),
            vmem((2, CH, D), F32),
            vmem((2, 2, CH, D), F32),
            vmem((2, 2, 2, CH, 512), BF16),
            vmem((6, 256, CH), BF16),
            vmem((6, 64, D), BF16),
            vmem((9, 64, 512), BF16),
            dma((7,)),
            dma((2, 2)),
            dma((2, 2)),
            dma((3,)),
            dma((3,)),
            dma((6, 2)),
            dma((6, 2)),
            dma((6,)),
            dma((6, 2, 2)),
            dma((6, 2)),
            dma((4, 2)),
            dma((3, 2, 2)),
            dma((9,)),
            dma((2,)),
            dma((6,)),
            dma((6,)),
            dma((9,)),
            dma((9,)),
            dma((2,)),
            dma((2,)),
            dma((2,)),
        ],
        compiler_params=pltpu.CompilerParams(
            collective_id=0, has_side_effects=True, vmem_limit_bytes=50 * 2**20
        ),
        cost_estimate=pl.CostEstimate(
            flops=13_153_337_344, bytes_accessed=12 * 2**20, transcendentals=2 * 4 * MB * HID
        ),
    )(fwd_in, bwd_in, cotangent, w_in, w_out)


def solution(mesh):
    in_specs = (
        P(("blk", "rep"), None),
        P(("blk", "rep"), None),
        P(("blk", "rep"), None),
        P(None, "blk"),
        P("blk", None),
    )
    out_specs = (P(("blk", "rep"), None), P(("blk", "rep"), None), P("rep", "blk"), P("blk", "rep"))
    return jax.shard_map(
        on_device, mesh=mesh, in_specs=in_specs, out_specs=out_specs, check_vma=False
    )
```

time: 148 us -> 142 us (0.959)
  Pallas kernels: 141 us -> 134 us
    pallas_call x1, Pallas kernels: 141 us -> 134 us  [on_device(): pl.pallas_call(kernel, out_shape=(jax.ShapeDtypeStruct((MB, D), BF16), ja...]
    unnamed x10 -> x12, local copies, waits for them, and re-layouts: 6.37 us -> 7.4 us
where the time goes in v2:
time: 142 us
  Pallas kernels  134 us (94%)
  local copies, waits for them, and re-layouts  7.4 us (5%)
    pallas_call x1, Pallas kernels, on_device(): pl.pallas_call(kernel, out_shape=(jax.ShapeDtypeStruct((MB, D), BF16), ja...  134 us
    unnamed x12, local copies, waits for them, and re-layouts  7.4 us

profile of v2, /device:TPU:31, one launch (start us, length us, event | category | flops | bytes accessed | tf_op | source)
XLA Modules:
  0.0 142.0 jit_solution(16020019937882271887)
XLA Ops:
  0.6 0.0 copy-start
  0.6 1.2 copy-done
  1.8 0.0 copy-start.1
  1.8 1.2 copy-done.1
  3.0 134.0 %shard_map.84 = (bf16[448,1024]{1,0:T(8,128)(2,1)S(1)}, bf16[448,1024]{1,0:T(8,128)(2,1)S(1)}, f32[512,512]{1,0:T(8,128)}, f32[512,512]{1,0:T(8,128)}) custom-call(bf16[448,1024]{1,0:T(8,128)(2,1)S(1)} %copy-done, bf16[448,1024]{1,0:T(8,128)(2,1)S(1)} %copy-done.1, bf16[448,1024]{1,0:T(8,128)(2,1)} %cot_hbm.1, bf16[1024,512]{1,0:T(8,128)(2,1)} %win_hbm.1, ...), custom_call_target="tpu_custom_call" | custom-call | flops 13153337344 | bytes 12582912 | tf_op jit(solution)/shard_map/pallas_call | solution.py:466
  137.0 0.9 copy.13
  137.9 0.0 copy-start.3
  137.9 0.9 copy.14
  138.8 0.6 copy-done.3
  139.5 0.0 copy-start.2
  139.5 1.0 copy.15
  140.4 0.6 copy-done.2
  141.1 1.0 copy.16
Async XLA Ops:
  0.6 1.2 copy-start
  1.8 1.2 copy-start.1
  137.9 1.6 %copy-start.3 = (f32[512,512]{1,0:T(8,128)S(1)}, f32[512,512]{1,0:T(8,128)}, u32[]{:S(2)}) copy-start(f32[512,512]{1,0:T(8,128)} %get-tuple-element.10) | copy-start | bytes 3145732
  139.5 1.6 %copy-start.2 = (f32[512,512]{1,0:T(8,128)S(1)}, f32[512,512]{1,0:T(8,128)}, u32[]{:S(2)}) copy-start(f32[512,512]{1,0:T(8,128)} %get-tuple-element.11) | copy-start | bytes 3145732

commit v3 on v2

--- a/solution.py
+++ b/solution.py
@@ -127,9 +127,9 @@
                 device_id=peer, device_id_type=MESH),
         )
 
-    STREAM_F = {0: (None, (0, 768), None), 1: (0, (768, 256), (0, 32)), 2: (12, None, (32, 64)),
-                3: (3, None, (96, 32))}
-    STREAM_B = {0: (None, 0, 0), 1: (15, 0, 64), 2: (3, 1, 0), 3: (12, 1, 64)}
+    STREAM_F = {0: (None, (0, 512), None), 1: (0, (512, 512), (0, 32)), 2: (12, None, (32, 48)),
+                3: (3, None, (80, 48))}
+    STREAM_B = {0: (None, 0, 0, 64), 1: (15, 0, 64, 64), 2: (3, 1, 0, 64), 3: (12, 1, 64, 64)}
 
     def pieces_w(n, s):
         _, rows_i, rows_o = STREAM_F[s]
@@ -221,8 +221,11 @@
         return [(2 * kind - 2 + h, lrecv.at[2 - kind, h], l_sem.at[2 - kind], core) for h in range(2)]
 
     def piece_g(ref, s):
-        _, a, row = STREAM_B[s]
-        return ref.at[a, pl.ds(row, 64)]
+        _, a, row, size = STREAM_B[s]
+        return ref.at[a, pl.ds(row, size)]
+
+    def held_g(slot, s):
+        return rly_b.at[slot, pl.ds(0, STREAM_B[s][3])]
 
     def send_g(i):
         for slot, dst, sem, core_ in parts_g(i):
@@ -240,17 +243,17 @@
                         remote(piece_g(gs.at[slot], s), piece_g(dst, s), xm_send.at[slot], sem,
                                dev).start()
                     else:
-                        remote(piece_g(gs.at[slot], s), rly_b.at[slot], xm_send.at[slot],
+                        remote(piece_g(gs.at[slot], s), held_g(slot, s), xm_send.at[slot],
                                rb_recv.at[slot], in_plane(via)).start()
 
     def relays_g(i):
         for slot, dst, sem, core_ in parts_g(i):
             dev = at(zhi * 16 - 1, core_, rep)
-            for s, (via, _, _) in STREAM_B.items():
+            for s, (via, _, _, _) in STREAM_B.items():
                 if via is not None:
                     yield via, (
-                        remote(rly_b.at[slot], rly_b.at[slot], rb_send.at[slot], rb_recv.at[slot], dev),
-                        remote(rly_b.at[slot], piece_g(dst, s), rb_send.at[slot], sem, dev),
+                        remote(held_g(slot, s), held_g(slot, s), rb_send.at[slot], rb_recv.at[slot], dev),
+                        remote(held_g(slot, s), piece_g(dst, s), rb_send.at[slot], sem, dev),
                     )
 
     def pass_g(i):
@@ -460,10 +463,15 @@
                 own_copy(n, h).wait_send()
 
 
+def hand_on(a, b, c, d, ao, bo, co, do):
+    for src, dst in ((a, ao), (b, bo), (c, co), (d, do)):
+        dst[...] = src[...]
+
+
 def on_device(fwd_in, bwd_in, cotangent, w_in, w_out):
     dma = pltpu.SemaphoreType.DMA
     vmem = pltpu.VMEM
-    return pl.pallas_call(
+    results = pl.pallas_call(
         kernel,
         out_shape=(
             jax.ShapeDtypeStruct((MB, D), BF16),
@@ -492,9 +500,9 @@
             vmem((2, CH, D), F32),
             vmem((2, 2, CH, D), F32),
             vmem((2, 2, 2, CH, 512), BF16),
-            vmem((6, 256, CH), BF16),
+            vmem((6, 512, CH), BF16),
             vmem((6, 64, D), BF16),
-            vmem((9, 64, 512), BF16),
+            vmem((9, 96, 512), BF16),
             dma((7,)),
             dma((2, 2)),
             dma((2, 2)),
@@ -518,12 +526,24 @@
             dma((2,)),
         ],
         compiler_params=pltpu.CompilerParams(
-            collective_id=0, has_side_effects=True, vmem_limit_bytes=50 * 2**20
+            collective_id=0, has_side_effects=True, vmem_limit_bytes=60 * 2**20
         ),
         cost_estimate=pl.CostEstimate(
             flops=13_153_337_344, bytes_accessed=12 * 2**20, transcendentals=2 * 4 * MB * HID
         ),
     )(fwd_in, bwd_in, cotangent, w_in, w_out)
+    steps = 4
+    blocks = [
+        pl.BlockSpec((r.shape[0] // steps, r.shape[1]), lambda step: (step, 0)) for r in results
+    ]
+    return pl.pallas_call(
+        hand_on,
+        grid=(steps,),
+        out_shape=tuple(jax.ShapeDtypeStruct(r.shape, r.dtype) for r in results),
+        in_specs=blocks,
+        out_specs=blocks,
+        compiler_params=pltpu.CompilerParams(vmem_limit_bytes=60 * 2**20),
+    )(*results)
 
 
 def solution(mesh):

time: 142 us -> 136 us (0.958)
  local copies, waits for them, and re-layouts: 7.4 us -> 0 us
  Pallas kernels: 134 us -> 136 us
    unnamed x12 -> x0, local copies, waits for them, and re-layouts: 7.4 us -> none
    pallas_call x0 -> x1, Pallas kernels: none -> 4.62 us  [on_device(): pl.pallas_call(hand_on, grid=(steps,), out_shape=tuple((jax.ShapeDtypeStr...]
    pallas_call x1, Pallas kernels: 134 us -> 131 us  [on_device(): pl.pallas_call(kernel, out_shape=(jax.ShapeDtypeStruct((MB, D), BF16), ja...]
where the time goes in v3:
time: 136 us
  Pallas kernels  136 us (100%)
    pallas_call x1, Pallas kernels, on_device(): pl.pallas_call(kernel, out_shape=(jax.ShapeDtypeStruct((MB, D), BF16), ja...  131 us
    pallas_call x1, Pallas kernels, on_device(): pl.pallas_call(hand_on, grid=(steps,), out_shape=tuple((jax.ShapeDtypeStr...  4.62 us

profile of v3, /device:TPU:31, one launch (start us, length us, event | category | flops | bytes accessed | tf_op | source)
XLA Modules:
  0.0 136.3 jit_solution(13847191196835232736)
XLA Ops:
  0.6 131.0 %shard_map.84 = (bf16[448,1024]{1,0:T(8,128)(2,1)}, bf16[448,1024]{1,0:T(8,128)(2,1)}, f32[512,512]{1,0:T(8,128)}, f32[512,512]{1,0:T(8,128)}) custom-call(bf16[448,1024]{1,0:T(8,128)(2,1)} %fwd_hbm.1, bf16[448,1024]{1,0:T(8,128)(2,1)} %bwd_hbm.1, bf16[448,1024]{1,0:T(8,128)(2,1)} %cot_hbm.1, bf16[1024,512]{1,0:T(8,128)(2,1)} %win_hbm.1, ...), custom_call_target="tpu_custom_call" | custom-call | flops 13153337344 | bytes 12582912 | tf_op jit(solution)/shard_map/pallas_call | solution.py:474
  131.7 4.6 %shard_map.85 = (bf16[448,1024]{1,0:T(8,128)(2,1)}, bf16[448,1024]{1,0:T(8,128)(2,1)}, f32[512,512]{1,0:T(8,128)}, f32[512,512]{1,0:T(8,128)}) custom-call(bf16[448,1024]{1,0:T(8,128)(2,1)} %get-tuple-element.8.a, bf16[448,1024]{1,0:T(8,128)(2,1)} %get-tuple-element.9.b, f32[512,512]{1,0:T(8,128)} %get-tuple-element.10.c, f32[512,512]{1,0:T(8,128)} %get-tuple-element.11.d), custom_call_target="tpu_custom_call" | custom-call | tf_op jit(solution)/shard_map/pallas_call | solution.py:539

commit v4 on v3

--- a/solution.py
+++ b/solution.py
@@ -329,7 +329,7 @@
         compute(n, n // 2, 2)
         for h in range(2):
             hand_out(n, h, halves(grad, h))
-    pass_w(P1C0)
+        pass_w(P1C0 if n == 1 else P1C1)
 
     def own_step(j, carry):
         compute(2 * j, j, 2)
@@ -337,7 +337,6 @@
         return carry
 
     lax.fori_loop(0, 2, own_step, 0)
-    pass_w(P1C1)
 
     def merge_own(j):
         remote(lrecv.at[j], lrecv.at[j], z_send.at[0], l_sem.at[j], ahead).wait_recv()
@@ -532,7 +531,7 @@
             flops=13_153_337_344, bytes_accessed=12 * 2**20, transcendentals=2 * 4 * MB * HID
         ),
     )(fwd_in, bwd_in, cotangent, w_in, w_out)
-    steps = 4
+    steps = 2
     blocks = [
         pl.BlockSpec((r.shape[0] // steps, r.shape[1]), lambda step: (step, 0)) for r in results
     ]

time: 136 us -> 135 us (level)
  Pallas kernels: 136 us -> 134 us
where the time goes in v4:
time: 135 us; the launch traced here: 134 us
  Pallas kernels  134 us (99%)
    pallas_call x1, Pallas kernels, on_device(): pl.pallas_call(kernel, out_shape=(jax.ShapeDtypeStruct((MB, D), BF16), ja...  130 us
    pallas_call x1, Pallas kernels, on_device(): pl.pallas_call(hand_on, grid=(steps,), out_shape=tuple((jax.ShapeDtypeStr...  3.54 us

profile of v4, /device:TPU:31, one launch (start us, length us, event | category | flops | bytes accessed | tf_op | source)
XLA Modules:
  0.0 134.4 jit_solution(17567537102085207686)
XLA Ops:
  0.6 130.3 %shard_map.84 = (bf16[448,1024]{1,0:T(8,128)(2,1)}, bf16[448,1024]{1,0:T(8,128)(2,1)}, f32[512,512]{1,0:T(8,128)}, f32[512,512]{1,0:T(8,128)}) custom-call(bf16[448,1024]{1,0:T(8,128)(2,1)} %fwd_hbm.1, bf16[448,1024]{1,0:T(8,128)(2,1)} %bwd_hbm.1, bf16[448,1024]{1,0:T(8,128)(2,1)} %cot_hbm.1, bf16[1024,512]{1,0:T(8,128)(2,1)} %win_hbm.1, ...), custom_call_target="tpu_custom_call" | custom-call | flops 13153337344 | bytes 12582912 | tf_op jit(solution)/shard_map/pallas_call | solution.py:473
  130.9 3.5 %shard_map.85 = (bf16[448,1024]{1,0:T(8,128)(2,1)}, bf16[448,1024]{1,0:T(8,128)(2,1)}, f32[512,512]{1,0:T(8,128)}, f32[512,512]{1,0:T(8,128)}) custom-call(bf16[448,1024]{1,0:T(8,128)(2,1)} %get-tuple-element.8.a, bf16[448,1024]{1,0:T(8,128)(2,1)} %get-tuple-element.9.b, f32[512,512]{1,0:T(8,128)} %get-tuple-element.10.c, f32[512,512]{1,0:T(8,128)} %get-tuple-element.11.d), custom_call_target="tpu_custom_call" | custom-call | tf_op jit(solution)/shard_map/pallas_call | solution.py:538
